TPU v7x, 256 devices: a whole 4x4x8 slice. The times are simulated.
256 devices in a mesh: ctx: 32 (over y, z), tp: 8 (over x, core).
Axes of the slice: x: 4, y: 4, z: 8, core: 2. Of those that a mesh axis runs over, the one named last changes fastest.
Arguments:
- context_block_rows: bfloat16 [16384, 8192], P('ctx', 'tp'), may hold values from -16 to 16
- query_hidden_rows: bfloat16 [64, 8192], P(None, 'tp'), may hold values from -16 to 16
- query_token_positions: int32 [64], replicated, may hold values from 16384 to 16573, as said below
- query_bound: int32 [64], replicated, may hold values from 1 to 16384, as said below
- query_matrix: bfloat16 [8192, 8192], P('ctx', 'tp'), may hold values from -0.0625 to 0.0625
- key_matrix: bfloat16 [8192, 1024], P('ctx', 'tp'), may hold values from -0.0625 to 0.0625
- value_matrix: bfloat16 [8192, 1024], P('ctx', 'tp'), may hold values from -0.0625 to 0.0625
Outputs:
- block_out: bfloat16 [16384, 8192], P('ctx', 'tp')
- query_out: bfloat16 [64, 8192], P(None, 'tp')
Inputs may be any that keep to these rules, and one draw needn't show every extreme that they name: query_token_positions rise strictly with the index; the first is 16384 and the last 16573. `query_bound`: some query token sees all 16384 context tokens.
All inputs are finite; a program needn't handle non-finite values.
Results may differ from a plain program's by a relative error of at most 0.0059.
The roundings to bfloat16 on the way count: a program that leaves them out, or rounds other values in their place, can miss the bound.
Values may be sent and summed in bfloat16 or wider, within the bound.
A program may use at most 128 MiB of HBM per device.

v0:
```python
import math
import jax
import jax.numpy as jnp
from jax import lax
from jax.sharding import PartitionSpec as P

HEAD_SIZE = 128


def from_root(value, axis, source):
    kept = jnp.where(lax.axis_index(axis) == source, value, 0).astype(value.dtype)
    return lax.psum(kept, axis)


def rope_table(half):
    values = []
    for index in range(half):
        freq = 500000.0 ** (-2.0 * index / (2.0 * half))
        wavelen = 2.0 * math.pi / freq
        if wavelen > 8192.0:
            values.append(freq / 8.0)
        elif wavelen < 2048.0:
            values.append(freq)
        else:
            smooth = (8192.0 / wavelen - 1.0) / 3.0
            values.append((1.0 - smooth) * freq / 8.0 + smooth * freq)
    return values


def apply_rotary(values, token_positions):
    half = values.shape[-1] // 2
    freqs = jnp.asarray(rope_table(half), jnp.float32)
    angle = token_positions.astype(jnp.float32)[:, None] * freqs[None, :]
    cosine = jnp.cos(angle)[:, None, :]
    sine = jnp.sin(angle)[:, None, :]
    first = values[..., :half]
    second = values[..., half:]
    return jnp.concatenate([first * cosine - second * sine, second * cosine + first * sine], -1)


def attend(query_heads_split, keys, values, valid):
    scale = 1.0 / math.sqrt(query_heads_split.shape[-1])
    scores = (
        jnp.einsum("qkgd,skd->qkgs", query_heads_split, keys, preferred_element_type=jnp.float32)
        * scale
    )
    scores = jnp.where(valid[:, None, None, :], scores, -1e30)
    peak = jnp.max(scores, -1)
    weights = jnp.exp(scores - peak[..., None])
    total = jnp.sum(weights, -1)
    mixed = jnp.einsum(
        "qkgs,skd->qkgd", weights.astype(jnp.bfloat16), values, preferred_element_type=jnp.float32
    )
    return (peak, total, mixed)


def on_device(
    context_block_rows,
    query_hidden_rows,
    query_token_positions,
    query_bound,
    query_matrix,
    key_matrix,
    value_matrix,
):
    ctx_index = lax.axis_index("ctx")
    blk = context_block_rows.shape[0]
    qcount = query_hidden_rows.shape[0]
    heads_q = query_matrix.shape[1] // HEAD_SIZE
    heads_kv = key_matrix.shape[1] // HEAD_SIZE
    head_group = heads_q // heads_kv
    whole_rows, whole_query = (
        lax.all_gather(context_block_rows, "tp", axis=1, tiled=True),
        lax.all_gather(query_hidden_rows, "tp", axis=1, tiled=True),
    )
    stacked = jnp.concatenate([whole_rows, whole_query], 0)
    head_rows = blk + qcount
    proj_query = jnp.dot(
        stacked,
        lax.all_gather(query_matrix, "ctx", axis=0, tiled=True),
        preferred_element_type=jnp.float32,
    )
    proj_key = jnp.dot(
        stacked,
        lax.all_gather(key_matrix, "ctx", axis=0, tiled=True),
        preferred_element_type=jnp.float32,
    )
    proj_value = jnp.dot(
        stacked,
        lax.all_gather(value_matrix, "ctx", axis=0, tiled=True),
        preferred_element_type=jnp.float32,
    )
    local_pos = ctx_index * blk + jnp.arange(blk, dtype=jnp.int32)
    k_block = apply_rotary(proj_key[:blk].reshape(blk, heads_kv, HEAD_SIZE), local_pos).astype(
        jnp.bfloat16
    )
    v_block = proj_value[:blk].reshape(blk, heads_kv, HEAD_SIZE).astype(jnp.bfloat16)
    key_token_rows = apply_rotary(
        proj_key[blk:head_rows].reshape(qcount, heads_kv, HEAD_SIZE), query_token_positions
    ).astype(jnp.bfloat16)
    value_token_rows = (
        proj_value[blk:head_rows].reshape(qcount, heads_kv, HEAD_SIZE).astype(jnp.bfloat16)
    )
    anchor_key, anchor_value = (from_root(k_block, "ctx", 0), from_root(v_block, "ctx", 0))
    q_block = apply_rotary(proj_query[:blk].reshape(blk, heads_q, HEAD_SIZE), local_pos).astype(
        jnp.bfloat16
    )
    query_token_rows = (
        apply_rotary(proj_query[blk:].reshape(qcount, heads_q, HEAD_SIZE), query_token_positions)
        .astype(jnp.bfloat16)
        .reshape(qcount, heads_kv, head_group, HEAD_SIZE)
    )
    keys_cat = jnp.concatenate([anchor_key, k_block], 0)
    values_cat = jnp.concatenate([anchor_value, v_block], 0)
    anchor_live = ctx_index > 0
    rows_step = min(blk, 512)
    rows_here = 0 + jnp.arange(rows_step, dtype=jnp.int32)
    valid = jnp.concatenate(
        [
            jnp.broadcast_to(anchor_live, (rows_step, blk)),
            rows_here[:, None] >= jnp.arange(blk, dtype=jnp.int32)[None, :],
        ],
        1,
    )
    query_heads_split = q_block.reshape(rows_step, heads_kv, head_group, HEAD_SIZE)
    peak, total, mixed = attend(query_heads_split, keys_cat, values_cat, valid)
    outputs = (
        (mixed / total[..., None]).astype(jnp.bfloat16).reshape(rows_step, heads_q * HEAD_SIZE)
    )
    valid_ctx = local_pos[None, :] < query_bound[:, None]
    peak, total, mixed = attend(query_token_rows, k_block, v_block, valid_ctx)
    top = lax.pmax(peak, "ctx")
    scaled = jnp.exp(peak - top)
    total_all, mixed_all = lax.psum((total * scaled, mixed * scaled[..., None]), "ctx")
    own = jnp.arange(qcount, dtype=jnp.int32)
    self_peak, self_total, self_mixed = attend(
        query_token_rows, key_token_rows, value_token_rows, own[:, None] >= own[None, :]
    )
    final = jnp.maximum(top, self_peak)
    w_ctx = jnp.exp(top - final)
    w_self = jnp.exp(self_peak - final)
    query_out = (mixed_all * w_ctx[..., None] + self_mixed * w_self[..., None]) / (
        total_all * w_ctx + self_total * w_self
    )[..., None]
    query_out = query_out.astype(jnp.bfloat16).reshape(qcount, heads_q * HEAD_SIZE)
    return (outputs, query_out)


def solution(mesh):
    placed = (
        P("ctx", "tp"),
        P(None, "tp"),
        P(),
        P(),
        P("ctx", "tp"),
        P("ctx", "tp"),
        P("ctx", "tp"),
    )
    return jax.shard_map(
        on_device,
        mesh=mesh,
        in_specs=placed,
        out_specs=(P("ctx", "tp"), P(None, "tp")),
        check_vma=False,
    )
```

profile of v0, /device:TPU:2, one launch (start us, length us, event | category | flops | bytes accessed | tf_op | source)
XLA Modules:
  0.0 689.7 jit_solution(3943614140132584248)
XLA Ops:
  12.3 1.4 broadcast_compare_fusion
  14.5 2.5 multiply_cosine_fusion
  17.0 47.3 %all-gather.6.cloned.1.call-done = bf16[512,8192]{1,0:T(8,128)(2,1)} async-done(((bf16[512,1024]{1,0:T(8,128)(2,1)}), bf16[512,8192]{1,0:T(8,128)(2,1)}) %all-gather.6.cloned.1.call-update) | async-done | bytes 8388624 | tf_op jit(solution)/shard_map/all_gather | solution.py:73
  64.3 7.6 %constant_dynamic-update-slice_fusion.1 = bf16[576,8192]{1,0:T(8,128)(2,1)} fusion(bf16[512,8192]{1,0:T(8,128)(2,1)} %all-gather.6.cloned.1.call-done), kind=kLoop, calls=%fused_computation.100 | loop fusion | bytes 16777216
  71.9 19.5 %all-gather.8.cloned.1.call-done = bf16[64,8192]{1,0:T(8,128)(2,1)} async-done(((bf16[64,1024]{1,0:T(8,128)(2,1)}), bf16[64,8192]{1,0:T(8,128)(2,1)}) %all-gather.8.cloned.1.call-update) | async-done | bytes 1048592 | tf_op jit(solution)/shard_map/all_gather | solution.py:74
  91.4 2.3 constant_dynamic-update-slice_fusion
  93.7 79.8 %all-gather.12.cloned.1.call-done = bf16[8192,128]{1,0:T(8,128)(2,1)} async-done(((bf16[256,128]{1,0:T(8,128)(2,1)}), bf16[8192,128]{1,0:T(8,128)(2,1)}) %all-gather.12.cloned.1.call-update) | async-done | bytes 2097168 | tf_op jit(solution)/shard_map/all_gather | solution.py:85
  173.5 5.8 fusion.83
  182.2 68.9 %all-gather.10.cloned.1.call-done = bf16[8192,128]{1,0:T(8,128)(2,1)} async-done(((bf16[256,128]{1,0:T(8,128)(2,1)}), bf16[8192,128]{1,0:T(8,128)(2,1)}) %all-gather.10.cloned.1.call-update) | async-done | bytes 2097168 | tf_op jit(solution)/shard_map/all_gather | solution.py:90
  251.1 6.9 convolution_convert_fusion
  258.9 132.5 %all-gather.14.cloned.1.call-done = bf16[8192,1024]{1,0:T(8,128)(2,1)} async-done(((bf16[256,1024]{1,0:T(8,128)(2,1)}), bf16[8192,1024]{1,0:T(8,128)(2,1)}) %all-gather.14.cloned.1.call-update) | async-done | bytes 16777232 | tf_op jit(solution)/shard_map/all_gather | solution.py:80
  391.4 14.9 %fusion.84 = f32[576,1024]{1,0:T(8,128)S(1)} fusion(bf16[576,8192]{1,0:T(8,128)(2,1)} %constant_dynamic-update-slice_fusion, bf16[8192,1024]{1,0:T(8,128)(2,1)} %all-gather.14.cloned.1.call-done), kind=kOutput, calls=%fused_computation.126 | convolution fusion | flops 9663676416 | bytes 28573696 | tf_op jit(solution)/shard_map/dot_general | solution.py:78
  406.8 1.4 fusion.81
  409.1 71.4 %pmax.7 = f32[64,1,8]{0,2,1:T(8,128)S(1)} all-reduce(f32[64,1,8]{0,2,1:T(8,128)S(1)} %bitcast.169), channel_id=1, replica_groups=mesh['ctx'=32,'tp'=8] {'ctx'}, use_global_device_ids=true, to_apply=%region_5.6 | all-reduce | flops 512 | bytes 4096 | tf_op jit(solution)/shard_map/pmax | solution.py:132
  481.1 2.0 fusion.79
  484.8 3.5 subtract_convert_fusion
  488.2 47.8 %all-reduce.7.cloned.1.call-done = (bf16[512,1,128]{2,0,1:T(8,128)(2,1)}, bf16[512,1,128]{2,0,1:T(8,128)(2,1)}) async-done(((bf16[512,1,128]{2,0,1:T(8,128)(2,1)}, bf16[512,1,128]{2,0,1:T(8,128)(2,1)}), (bf16[512,1,128]{2,0,1:T(8,128)(2,1)}, bf16[512,1,128]{2,0,1:T(8,128)(2,1)})) %all-reduce.7.cloned.1.call-update) | async-done | bytes 262160 | tf_op jit(solution)/shard_map/psum | solution.py:12
  536.1 10.7 %fusion.2 = (f32[512,8]{0,1:T(8,128)S(1)}, f32[1024,512,8]{1,0,2:T(8,128)}) fusion(pred[512,1024]{0,1:T(8,128)(4,1)} %concatenate.62, bf16[512,8,64]{2,0,1:T(8,128)(2,1)} %get-tuple-element.9, bf16[512,8,64]{2,0,1:T(8,128)(2,1)S(1)} %get-tuple-element.8, bf16[512,1,64]{2,0,1:T(8,128)(2,1)} %copy-done.1, bf16[512,1,64]{2,0,1:T(8,128)(2,1)S(1)} %get-tuple-element.14, ...), kind=kOutput, calls=%fused_computation.4 | convolution fusion | flops 1089204224 | bytes 18628608 | tf_op jit(solution)/shard_map/qkgd,skd->qkgs/dot_general | solution.py:44
  546.8 9.3 %fusion = f32[512,8]{0,1:T(8,128)S(1)} fusion(f32[1024,512,8]{1,0,2:T(8,128)} %get-tuple-element.32, f32[512,8]{0,1:T(8,128)S(1)} %get-tuple-element.31, pred[512,1024]{0,1:T(8,128)(4,1)S(1)} %copy-done), kind=kLoop, calls=%fused_computation.2 | loop fusion | flops 16773120 | bytes 17334272 | tf_op jit(solution)/shard_map/reduce_sum | solution.py:50
  556.5 9.1 %fusion.7 = bf16[1,128,512,8]{2,1,3,0:T(8,128)(2,1)S(1)} fusion(f32[1024,512,8]{1,0,2:T(8,128)} %get-tuple-element.32, f32[512,8]{0,1:T(8,128)S(1)} %get-tuple-element.31, pred[512,1024]{0,1:T(8,128)(4,1)S(1)} %copy-done, f32[512,8]{0,1:T(8,128)S(1)} %fusion, bf16[512,1,128]{2,0,1:T(8,128)(2,1)S(1)} %copy-done.4, bf16[512,1,128]{2,0,1:T(8,128)(2,1)S(1)} %copy-done.10), kind=kOutput, calls=%fused_computation.10 | convolution fusion | flops 1092091904 | bytes 18644992 | tf_op jit(solution)/shard_map/qkgs,skd->qkgd/dot_general | solution.py:51
  565.7 1.3 copy.29
  567.0 72.5 %psum.31 = f32[64,1,8]{0,2,1:T(8,128)S(1)} all-reduce(f32[64,1,8]{0,2,1:T(8,128)S(1)} %copy-done.8), channel_id=1, replica_groups=mesh['ctx'=32,'tp'=8] {'ctx'}, use_global_device_ids=true, to_apply=%region_9.10 | all-reduce | flops 512 | bytes 4096 | tf_op jit(solution)/shard_map/psum | solution.py:134
  639.5 41.2 %all-reduce.5.cloned.1.call-done = f32[64,1,8,128]{3,0,2,1:T(8,128)} async-done(((f32[64,1,8,128]{3,0,2,1:T(8,128)}), f32[64,1,8,128]{3,0,2,1:T(8,128)}) %all-reduce.5.cloned.1.call-update) | async-done | bytes 262160 | tf_op jit(solution)/shard_map/psum | solution.py:134
  680.7 1.3 fusion.19
  (63 shorter events, 14.3 us)
Async XLA Ops:
  7.2 57.1 %all-gather.6.cloned.1.call-start = ((), (), s32[]{:S(2)}) async-start(), calls=%async_computation | async-start | bytes 9437184 | tf_op jit(solution)/shard_map/all_gather | solution.py:73
  7.9 83.5 %all-gather.8.cloned.1.call-start = ((), (), s32[]{:S(2)}) async-start(), calls=%async_computation.1 | async-start | bytes 1179648 | tf_op jit(solution)/shard_map/all_gather | solution.py:74
  8.6 164.9 %all-gather.12.cloned.1.call-start = ((), (), s32[]{:S(2)}) async-start(), calls=%async_computation.3 | async-start | bytes 2162688 | tf_op jit(solution)/shard_map/all_gather | solution.py:85
  9.4 241.7 %all-gather.10.cloned.1.call-start = ((), (), s32[]{:S(2)}) async-start(), calls=%async_computation.2 | async-start | bytes 2162688 | tf_op jit(solution)/shard_map/all_gather | solution.py:90
  10.0 381.4 %all-gather.14.cloned.1.call-start = ((), (), s32[]{:S(2)}) async-start(), calls=%async_computation.4 | async-start | bytes 17301504 | tf_op jit(solution)/shard_map/all_gather | solution.py:80
  10.5 525.5 %all-reduce.7.cloned.1.call-start = ((), (), s32[]{:S(2)}) async-start(), calls=%async_computation.6 | async-start | bytes 524288 | tf_op jit(solution)/shard_map/psum | solution.py:12
  71.9 107.5 %copy-start.9 = (f32[64]{0:T(128)S(1)}, f32[64]{0:T(128)}, u32[]{:S(2)}) copy-start(f32[64]{0:T(128)} %constant.24.clone) | copy-start | bytes 772
  180.6 225.7 %copy-start.1 = (bf16[512,1,64]{2,0,1:T(8,128)(2,1)}, bf16[512,1,64]{2,0,1:T(8,128)(2,1)S(1)}, u32[]{:S(2)}) copy-start(bf16[512,1,64]{2,0,1:T(8,128)(2,1)S(1)} %get-tuple-element.15) | copy-start | bytes 196612
  258.0 133.4 %copy-start.2 = (bf16[576,128]{1,0:T(8,128)(2,1)}, bf16[576,128]{1,0:T(8,128)(2,1)S(1)}, u32[]{:S(2)}) copy-start(bf16[576,128]{1,0:T(8,128)(2,1)S(1)} %convolution_convert_fusion) | copy-start | bytes 442372
  258.8 421.9 %all-reduce.5.cloned.1.call-start = ((), (), s32[]{:S(2)}) async-start(), calls=%async_computation.5 | async-start | bytes 524288 | tf_op jit(solution)/shard_map/psum | solution.py:134
  480.6 2.5 copy-start.7
  480.6 3.1 copy-start.3
  536.1 10.7 %copy-start = (pred[512,1024]{0,1:T(8,128)(4,1)S(1)}, pred[512,1024]{0,1:T(8,128)(4,1)}, u32[]{:S(2)}) copy-start(pred[512,1024]{0,1:T(8,128)(4,1)} %concatenate.62) | copy-start | bytes 1572868
  546.8 9.3 %copy-start.5 = (bf16[64,64]{1,0:T(8,128)(2,1)S(1)}, bf16[64,64]{1,0:T(8,128)(2,1)}, u32[]{:S(2)}) copy-start(bf16[64,64]{1,0:T(8,128)(2,1)} %get-tuple-element.20) | copy-start | bytes 24580
  546.8 9.3 %copy-start.6 = (bf16[64,64]{1,0:T(8,128)(2,1)S(1)}, bf16[64,64]{1,0:T(8,128)(2,1)}, u32[]{:S(2)}) copy-start(bf16[64,64]{1,0:T(8,128)(2,1)} %get-tuple-element.21) | copy-start | bytes 24580
  546.8 9.6 %copy-start.4 = (bf16[512,1,128]{2,0,1:T(8,128)(2,1)S(1)}, bf16[512,1,128]{2,0,1:T(8,128)(2,1)}, u32[]{:S(2)}) copy-start(bf16[512,1,128]{2,0,1:T(8,128)(2,1)} %get-tuple-element.18) | copy-start | bytes 393220
  546.8 9.6 %copy-start.10 = (bf16[512,1,128]{2,0,1:T(8,128)(2,1)S(1)}, bf16[512,1,128]{2,0,1:T(8,128)(2,1)}, u32[]{:S(2)}) copy-start(bf16[512,1,128]{2,0,1:T(8,128)(2,1)} %get-tuple-element.7) | copy-start | bytes 393220
  556.5 10.5 %copy-start.8 = (f32[64,1,8]{0,2,1:T(8,128)S(1)}, f32[64,1,8]{0,2,1:T(8,128)}, u32[]{:S(2)}) copy-start(f32[64,1,8]{0,2,1:T(8,128)} %get-tuple-element.25) | copy-start | bytes 6148
Sparse Core Ops, SparseCore 0:
  9.8 54.4 all-gather.5
  66.1 25.2 all-gather.7
  94.0 79.4 all-gather.11
  176.0 75.1 all-gather.9
  253.6 137.7 all-gather.13
  394.7 141.2 all-reduce.6
  539.5 141.1 all-reduce.4
where the time goes:
time: 690 us
  waiting for transfers between devices  440 us (64%)
  blocking collectives  144 us (21%)
  matrix products  51.5 us (7%)
  other arithmetic  23.5 us (3%)
  local copies, waits for them, and re-layouts  15.8 us (2%)
  between operations  14.4 us (2%)
    all_gather x1, waiting for transfers between devices, on_device(): lax.all_gather(query_matrix, 'ctx', axis=0, tiled=True)  133 us
    all_gather x1, waiting for transfers between devices, on_device(): lax.all_gather(key_matrix, 'ctx', axis=0, tiled=True)  79.8 us
    psum x1, blocking collectives, on_device(): lax.psum((total * scaled, mixed * scaled[..., None]), 'ctx')  72.5 us
    pmax x1, blocking collectives, on_device(): top = lax.pmax(peak, 'ctx')  71.4 us
    all_gather x1, waiting for transfers between devices, on_device(): lax.all_gather(value_matrix, 'ctx', axis=0, tiled=True)  68.9 us
    psum x1, waiting for transfers between devices, from_root(): return lax.psum(kept, axis)  47.8 us
    all_gather x1, waiting for transfers between devices, on_device(): lax.all_gather(context_block_rows, 'tp', axis=1, tiled=True)  47.3 us
    psum x1, waiting for transfers between devices, on_device(): lax.psum((total * scaled, mixed * scaled[..., None]), 'ctx')  41.2 us
  transfers between devices with their start and end apart: 7, of which 7 were waited for; matrix products, arithmetic and copies ran while one was open for 13% of the time, Pallas kernels for 0%

commit v1 on v0

--- a/solution.py
+++ b/solution.py
@@ -70,7 +70,10 @@
     heads_kv = key_matrix.shape[1] // HEAD_SIZE
     head_group = heads_q // heads_kv
     whole_rows, whole_query = (
-        lax.all_gather(context_block_rows, "tp", axis=1, tiled=True),
+        jnp.concatenate(
+            lax.all_to_all(jnp.stack([context_block_rows] * lax.axis_size("tp")), "tp", 0, 0),
+            axis=1,
+        ),
         lax.all_gather(query_hidden_rows, "tp", axis=1, tiled=True),
     )
     stacked = jnp.concatenate([whole_rows, whole_query], 0)

time: 690 us -> 652 us (0.945)
  waiting for transfers between devices: 440 us -> 398 us
  starting transfers between devices: 0.27 us -> 7.66 us
    all_gather x1 -> x0, waiting for transfers between devices: 47.3 us -> none  [on_device(): lax.all_gather(context_block_rows, 'tp', axis=1, tiled=True)]
    all_gather x1, waiting for transfers between devices: 19.5 us -> 27.5 us  [on_device(): lax.all_gather(query_hidden_rows, 'tp', axis=1, tiled=True)]
    all_to_all x0 -> x1, starting transfers between devices: none -> 7.28 us  [on_device(): lax.all_to_all(jnp.stack([context_block_rows] * lax.axis_size('tp')), 'tp...]
  transfers between devices with their start and end apart: 7 -> 7, of which waited for: 7 -> 6; matrix products, arithmetic and copies ran while one was open for 13% -> 13% of each run, Pallas kernels for 0% -> 0%
where the time goes in v1:
time: 652 us
  waiting for transfers between devices  398 us (61%)
  blocking collectives  144 us (22%)
  matrix products  54.5 us (8%)
  other arithmetic  20.8 us (3%)
  between operations  14.4 us (2%)
  local copies, waits for them, and re-layouts  13.2 us (2%)
  starting transfers between devices  7.66 us (1%)
    all_gather x1, waiting for transfers between devices, on_device(): lax.all_gather(query_matrix, 'ctx', axis=0, tiled=True)  132 us
    all_gather x1, waiting for transfers between devices, on_device(): lax.all_gather(key_matrix, 'ctx', axis=0, tiled=True)  80.8 us
    psum x1, blocking collectives, on_device(): lax.psum((total * scaled, mixed * scaled[..., None]), 'ctx')  72.5 us
    pmax x1, blocking collectives, on_device(): top = lax.pmax(peak, 'ctx')  71.3 us
    all_gather x1, waiting for transfers between devices, on_device(): lax.all_gather(value_matrix, 'ctx', axis=0, tiled=True)  67.3 us
    psum x1, waiting for transfers between devices, from_root(): return lax.psum(kept, axis)  46.9 us
    psum x1, waiting for transfers between devices, on_device(): lax.psum((total * scaled, mixed * scaled[..., None]), 'ctx')  41.1 us
    all_gather x1, waiting for transfers between devices, on_device(): lax.all_gather(query_hidden_rows, 'tp', axis=1, tiled=True)  27.5 us
  transfers between devices with their start and end apart: 7, of which 6 were waited for; matrix products, arithmetic and copies ran while one was open for 13% of the time, Pallas kernels for 0%

profile of v1, /device:TPU:2, one launch (start us, length us, event | category | flops | bytes accessed | tf_op | source)
XLA Modules:
  0.0 652.1 jit_solution(15494533580177052752)
XLA Ops:
  7.2 1.7 copy.22
  11.0 1.5 copy.21
  12.5 4.0 stack.2
  16.5 7.3 %all-to-all-start = ((bf16[8,512,1024]{1,2,0:T(8,128)(2,1)}), bf16[8,512,1024]{1,2,0:T(8,128)(2,1)}, u32[]{:S(2)}, u32[]{:S(2)}) async-start(bf16[8,512,1024]{1,2,0:T(8,128)(2,1)} %stack.2), calls=%async_computation | async-start | bytes 16777216 | tf_op jit(solution)/shard_map/all_to_all | solution.py:74
  25.7 1.8 multiply_cosine_fusion
  27.6 27.5 %all-gather.5.cloned.1.call-done = bf16[64,8192]{0,1:T(8,128)(2,1)} async-done(((bf16[64,1024]{0,1:T(8,128)(2,1)}), bf16[64,8192]{0,1:T(8,128)(2,1)}) %all-gather.5.cloned.1.call-update) | async-done | bytes 1048592 | tf_op jit(solution)/shard_map/all_gather | solution.py:77
  55.1 80.8 %all-gather.9.cloned.1.call-done = bf16[8192,128]{1,0:T(8,128)(2,1)} async-done(((bf16[256,128]{1,0:T(8,128)(2,1)}), bf16[8192,128]{1,0:T(8,128)(2,1)}) %all-gather.9.cloned.1.call-update) | async-done | bytes 2097168 | tf_op jit(solution)/shard_map/all_gather | solution.py:88
  135.9 7.6 %fusion.8 = f32[576,128]{1,0:T(8,128)S(1)} fusion(bf16[8192,128]{1,0:T(8,128)(2,1)} %all-gather.9.cloned.1.call-done, bf16[64,8192]{0,1:T(8,128)(2,1)} %all-gather.5.cloned.1.call-done, bf16[512,8192]{0,1:T(8,128)(2,1)} %bitcast.1), kind=kOutput, calls=%fused_computation.10 | convolution fusion | flops 1226833920 | bytes 11829248 | tf_op jit(solution)/shard_map/dot_general | solution.py:86
  146.4 67.3 %all-gather.7.cloned.1.call-done = bf16[8192,128]{1,0:T(8,128)(2,1)} async-done(((bf16[256,128]{1,0:T(8,128)(2,1)}), bf16[8192,128]{1,0:T(8,128)(2,1)}) %all-gather.7.cloned.1.call-update) | async-done | bytes 2097168 | tf_op jit(solution)/shard_map/all_gather | solution.py:93
  213.7 7.1 %fusion.22 = bf16[576,128]{1,0:T(8,128)(2,1)S(1)} fusion(bf16[8192,128]{1,0:T(8,128)(2,1)} %all-gather.7.cloned.1.call-done, bf16[64,8192]{0,1:T(8,128)(2,1)S(1)} %copy-done.11, bf16[512,8192]{0,1:T(8,128)(2,1)} %bitcast.1), kind=kOutput, calls=%fused_computation.30 | convolution fusion | flops 1226907648 | bytes 11681792 | tf_op jit(solution)/shard_map/dot_general | solution.py:91
  221.8 132.2 %all-gather.11.cloned.1.call-done = bf16[8192,1024]{1,0:T(8,128)(2,1)} async-done(((bf16[256,1024]{1,0:T(8,128)(2,1)}), bf16[8192,1024]{1,0:T(8,128)(2,1)}) %all-gather.11.cloned.1.call-update) | async-done | bytes 16777232 | tf_op jit(solution)/shard_map/all_gather | solution.py:83
  354.0 15.9 %fusion.7 = f32[576,1024]{1,0:T(8,128)S(1)} fusion(bf16[8192,1024]{1,0:T(8,128)(2,1)} %all-gather.11.cloned.1.call-done, bf16[64,8192]{0,1:T(8,128)(2,1)S(1)} %copy-done.11, bf16[512,8192]{0,1:T(8,128)(2,1)} %bitcast.1), kind=kOutput, calls=%fused_computation.9 | convolution fusion | flops 9682550784 | bytes 28573696 | tf_op jit(solution)/shard_map/dot_general | solution.py:81
  370.5 1.4 fusion.88
  372.8 71.3 %pmax.7 = f32[64,1,8]{0,2,1:T(8,128)S(1)} all-reduce(f32[64,1,8]{0,2,1:T(8,128)S(1)} %bitcast.169), channel_id=1, replica_groups=mesh['ctx'=32,'tp'=8] {'ctx'}, use_global_device_ids=true, to_apply=%region_5.6 | all-reduce | flops 512 | bytes 4096 | tf_op jit(solution)/shard_map/pmax | solution.py:135
  444.6 2.0 fusion.86
  448.3 3.5 subtract_convert_fusion
  451.8 46.9 %all-reduce.7.cloned.1.call-done = (bf16[512,1,128]{2,0,1:T(8,128)(2,1)}, bf16[512,1,128]{2,0,1:T(8,128)(2,1)}) async-done(((bf16[512,1,128]{2,0,1:T(8,128)(2,1)}, bf16[512,1,128]{2,0,1:T(8,128)(2,1)}), (bf16[512,1,128]{2,0,1:T(8,128)(2,1)}, bf16[512,1,128]{2,0,1:T(8,128)(2,1)})) %all-reduce.7.cloned.1.call-update) | async-done | bytes 262160 | tf_op jit(solution)/shard_map/psum | solution.py:12
  498.6 10.7 %fusion.2 = (f32[512,8]{0,1:T(8,128)S(1)}, f32[1024,512,8]{1,0,2:T(8,128)}) fusion(pred[512,1024]{0,1:T(8,128)(4,1)} %concatenate.62, bf16[512,8,64]{2,0,1:T(8,128)(2,1)} %get-tuple-element.9, bf16[512,8,64]{2,0,1:T(8,128)(2,1)S(1)} %get-tuple-element.8, bf16[512,1,64]{2,0,1:T(8,128)(2,1)} %copy-done.1, bf16[512,1,64]{2,0,1:T(8,128)(2,1)S(1)} %get-tuple-element.14, ...), kind=kOutput, calls=%fused_computation.4 | convolution fusion | flops 1089204224 | bytes 18628608 | tf_op jit(solution)/shard_map/qkgd,skd->qkgs/dot_general | solution.py:44
  509.4 9.3 %fusion = f32[512,8]{0,1:T(8,128)S(1)} fusion(f32[1024,512,8]{1,0,2:T(8,128)} %get-tuple-element.32, f32[512,8]{0,1:T(8,128)S(1)} %get-tuple-element.31, pred[512,1024]{0,1:T(8,128)(4,1)S(1)} %copy-done), kind=kLoop, calls=%fused_computation.2 | loop fusion | flops 16773120 | bytes 17334272 | tf_op jit(solution)/shard_map/reduce_sum | solution.py:50
  519.0 9.1 %fusion.10 = bf16[1,128,512,8]{2,1,3,0:T(8,128)(2,1)S(1)} fusion(f32[1024,512,8]{1,0,2:T(8,128)} %get-tuple-element.32, f32[512,8]{0,1:T(8,128)S(1)} %get-tuple-element.31, pred[512,1024]{0,1:T(8,128)(4,1)S(1)} %copy-done, f32[512,8]{0,1:T(8,128)S(1)} %fusion, bf16[512,1,128]{2,0,1:T(8,128)(2,1)S(1)} %copy-done.4, bf16[512,1,128]{2,0,1:T(8,128)(2,1)S(1)} %copy-done.12), kind=kOutput, calls=%fused_computation.14 | convolution fusion | flops 1092091904 | bytes 18644992 | tf_op jit(solution)/shard_map/qkgs,skd->qkgd/dot_general | solution.py:51
  528.2 1.3 copy.31
  529.5 72.5 %psum.31 = f32[64,1,8]{0,2,1:T(8,128)S(1)} all-reduce(f32[64,1,8]{0,2,1:T(8,128)S(1)} %copy-done.8), channel_id=1, replica_groups=mesh['ctx'=32,'tp'=8] {'ctx'}, use_global_device_ids=true, to_apply=%region_9.10 | all-reduce | flops 512 | bytes 4096 | tf_op jit(solution)/shard_map/psum | solution.py:137
  602.1 41.1 %all-reduce.5.cloned.1.call-done = f32[64,1,8,128]{3,0,2,1:T(8,128)} async-done(((f32[64,1,8,128]{3,0,2,1:T(8,128)}), f32[64,1,8,128]{3,0,2,1:T(8,128)}) %all-reduce.5.cloned.1.call-update) | async-done | bytes 262160 | tf_op jit(solution)/shard_map/psum | solution.py:137
  643.2 1.3 fusion.23
  (69 shorter events, 12.7 us)
Async XLA Ops:
  7.2 47.9 %all-gather.5.cloned.1.call-start = ((), (), s32[]{:S(2)}) async-start(), calls=%async_computation.1 | async-start | bytes 2359296 | tf_op jit(solution)/shard_map/all_gather | solution.py:77
  9.0 126.9 %all-gather.9.cloned.1.call-start = ((), (), s32[]{:S(2)}) async-start(), calls=%async_computation.3 | async-start | bytes 2162688 | tf_op jit(solution)/shard_map/all_gather | solution.py:88
  9.7 204.0 %all-gather.7.cloned.1.call-start = ((), (), s32[]{:S(2)}) async-start(), calls=%async_computation.2 | async-start | bytes 2162688 | tf_op jit(solution)/shard_map/all_gather | solution.py:93
  10.5 343.5 %all-gather.11.cloned.1.call-start = ((), (), s32[]{:S(2)}) async-start(), calls=%async_computation.4 | async-start | bytes 17301504 | tf_op jit(solution)/shard_map/all_gather | solution.py:83
  16.5 7.3 %copy-start.13 = (s32[64]{0:T(128)S(1)}, s32[64]{0:T(128)}, u32[]{:S(2)}) copy-start(s32[64]{0:T(128)} %param.13) | copy-start | bytes 772
  16.5 8.3 %copy-start.10 = (s32[64]{0:T(128)S(1)}, s32[64]{0:T(128)}, u32[]{:S(2)}) copy-start(s32[64]{0:T(128)} %param.14) | copy-start | bytes 772
  16.5 9.0 %copy-start.9 = (f32[64]{0:T(128)S(1)}, f32[64]{0:T(128)}, u32[]{:S(2)}) copy-start(f32[64]{0:T(128)} %constant.24.clone) | copy-start | bytes 772
  16.5 119.4 %all-to-all-start = ((bf16[8,512,1024]{1,2,0:T(8,128)(2,1)}), bf16[8,512,1024]{1,2,0:T(8,128)(2,1)}, u32[]{:S(2)}, u32[]{:S(2)}) async-start(bf16[8,512,1024]{1,2,0:T(8,128)(2,1)} %stack.2), calls=%async_computation | async-start | bytes 16777216 | tf_op jit(solution)/shard_map/all_to_all | solution.py:74
  23.8 474.9 %all-reduce.7.cloned.1.call-start = ((), (), s32[]{:S(2)}) async-start(), calls=%async_computation.6 | async-start | bytes 524288 | tf_op jit(solution)/shard_map/psum | solution.py:12
  135.9 77.8 %copy-start.11 = (bf16[64,8192]{0,1:T(8,128)(2,1)S(1)}, bf16[64,8192]{0,1:T(8,128)(2,1)}, u32[]{:S(2)}) copy-start(bf16[64,8192]{0,1:T(8,128)(2,1)} %all-gather.5.cloned.1.call-done) | copy-start | bytes 3145732
  144.8 76.0 %copy-start.1 = (bf16[512,1,64]{2,0,1:T(8,128)(2,1)}, bf16[512,1,64]{2,0,1:T(8,128)(2,1)S(1)}, u32[]{:S(2)}) copy-start(bf16[512,1,64]{2,0,1:T(8,128)(2,1)S(1)} %get-tuple-element.15) | copy-start | bytes 196612
  220.8 133.2 %copy-start.2 = (bf16[576,128]{1,0:T(8,128)(2,1)}, bf16[576,128]{1,0:T(8,128)(2,1)S(1)}, u32[]{:S(2)}) copy-start(bf16[576,128]{1,0:T(8,128)(2,1)S(1)} %fusion.22) | copy-start | bytes 442372
  221.5 421.6 %all-reduce.5.cloned.1.call-start = ((), (), s32[]{:S(2)}) async-start(), calls=%async_computation.5 | async-start | bytes 524288 | tf_op jit(solution)/shard_map/psum | solution.py:137
  444.1 2.5 copy-start.7
  444.1 3.1 copy-start.3
  498.6 10.7 %copy-start = (pred[512,1024]{0,1:T(8,128)(4,1)S(1)}, pred[512,1024]{0,1:T(8,128)(4,1)}, u32[]{:S(2)}) copy-start(pred[512,1024]{0,1:T(8,128)(4,1)} %concatenate.62) | copy-start | bytes 1572868
  509.3 9.3 %copy-start.5 = (bf16[64,64]{1,0:T(8,128)(2,1)S(1)}, bf16[64,64]{1,0:T(8,128)(2,1)}, u32[]{:S(2)}) copy-start(bf16[64,64]{1,0:T(8,128)(2,1)} %get-tuple-element.20) | copy-start | bytes 24580
  509.3 9.3 %copy-start.6 = (bf16[64,64]{1,0:T(8,128)(2,1)S(1)}, bf16[64,64]{1,0:T(8,128)(2,1)}, u32[]{:S(2)}) copy-start(bf16[64,64]{1,0:T(8,128)(2,1)} %get-tuple-element.21) | copy-start | bytes 24580
  509.3 9.6 %copy-start.4 = (bf16[512,1,128]{2,0,1:T(8,128)(2,1)S(1)}, bf16[512,1,128]{2,0,1:T(8,128)(2,1)}, u32[]{:S(2)}) copy-start(bf16[512,1,128]{2,0,1:T(8,128)(2,1)} %get-tuple-element.18) | copy-start | bytes 393220
  509.4 9.6 %copy-start.12 = (bf16[512,1,128]{2,0,1:T(8,128)(2,1)S(1)}, bf16[512,1,128]{2,0,1:T(8,128)(2,1)}, u32[]{:S(2)}) copy-start(bf16[512,1,128]{2,0,1:T(8,128)(2,1)} %get-tuple-element.7) | copy-start | bytes 393220
  519.0 10.5 %copy-start.8 = (f32[64,1,8]{0,2,1:T(8,128)S(1)}, f32[64,1,8]{0,2,1:T(8,128)}, u32[]{:S(2)}) copy-start(f32[64,1,8]{0,2,1:T(8,128)} %get-tuple-element.25) | copy-start | bytes 6148
Sparse Core Ops, SparseCore 0:
  10.4 44.5 all-gather.4
  57.7 78.2 all-gather.8
  138.5 75.1 all-gather.6
  216.1 137.7 all-gather.10
  357.3 141.2 all-reduce.6
  502.0 141.1 all-reduce.4
